TPU v7x, 32 devices: a whole 2x2x4 slice. The times are simulated.
32 devices in a mesh: group: 2 (over x), tp: 8 (over z, y), dp: 2 (over core).
Axes of the slice: x: 2, y: 2, z: 4, core: 2. Of those that a mesh axis runs over, the one named last changes fastest.
Arguments:
- gate_up: bfloat16 [4096, 2, 14336], P(('group', 'dp'), None, 'tp'), parts along dimension 0, may hold values from -6 to 6
- residual: bfloat16 [4096, 8192], P(('group', 'dp'), 'tp'), parts along dimension 0, may hold values from -40 to 40
- down_weight: bfloat16 [14336, 8192], P('tp'), may hold values from -0.046875 to 0.046875
- shrink_weight: bfloat16 [16, 14336, 64], P(None, 'tp'), may hold values from -0.046875 to 0.046875
- expand_weight: bfloat16 [16, 64, 8192], P(None, None, 'tp'), may hold values from -0.75 to 0.75
- block_adapter: int32 [128], P(('group', 'dp')), parts along dimension 0, may hold values from 0 to 15
- adapter_slot: int32 [16], replicated, may hold values from 0 to 15, each once
- norm_gain: bfloat16 [8192], P('tp'), may hold values from 0.099609375 to 1.8984375
Outputs:
- updated: bfloat16 [4096, 8192], P(('group', 'dp'), 'tp'), parts along dimension 0
- normed: bfloat16 [4096, 8192], P(('group', 'dp'), 'tp'), parts along dimension 0
There are 2 independent parts, one for each index of `group`. A program takes and returns all parts, laid end to end along the dimension named above; an argument that names none is the same for every part. Nothing has to cross between parts.
All inputs are finite; a program needn't handle non-finite values.
Results may differ from a plain program's by a relative error of at most 0.009.
Values may be sent and summed in bfloat16 or wider, within the bound.
A program may use at most 192 MiB of HBM per device.

v0:
```python
import jax
import jax.numpy as jnp
from jax import lax
from jax.sharding import PartitionSpec as P

MODEL_WIDTH = 8192


adapter_scale = 0.5


def on_device(
    gate_up,
    residual,
    down_weight,
    shrink_weight,
    expand_weight,
    block_adapter,
    adapter_slot,
    norm_gain,
):
    gate_val = gate_up[:, 0, :].astype(jnp.float32)
    up_val = gate_up[:, 1, :].astype(jnp.float32)
    hidden = (jax.nn.silu(gate_val) * up_val).astype(jnp.bfloat16)
    count_of_rows, ff_local = hidden.shape
    blocks = block_adapter.shape[0]
    block_rows = count_of_rows // blocks
    adapters = adapter_slot.shape[0]
    column_count = expand_weight.shape[2]
    adapter_range = jnp.arange(adapters, dtype=jnp.int32)
    chosen = block_adapter[:, None] == adapter_range[None, :]
    slot_ids = jnp.sum(jnp.where(chosen, adapter_slot[None, :], 0), axis=1)
    stacked = hidden.reshape(blocks, block_rows, ff_local)
    picked = shrink_weight[slot_ids]
    rank_terms = jnp.einsum("bkf,bfr->bkr", stacked, picked, preferred_element_type=jnp.float32)
    shrunk_rows = lax.psum(rank_terms.astype(jnp.bfloat16), "tp")
    base_term = jnp.dot(hidden, down_weight, preferred_element_type=jnp.float32)
    projection_sum = lax.psum_scatter(
        base_term.astype(jnp.bfloat16), "tp", scatter_dimension=1, tiled=True
    ).astype(jnp.float32)
    expand_selected = expand_weight[slot_ids]
    adapter_term = jnp.einsum(
        "xcf,xfe->xce", shrunk_rows, expand_selected, preferred_element_type=jnp.float32
    )
    adapter_term = adapter_term.reshape(count_of_rows, column_count)
    updated = (residual.astype(jnp.float32) + projection_sum + adapter_scale * adapter_term).astype(
        jnp.bfloat16
    )
    widened = updated.astype(jnp.float32)
    square_tot = lax.psum(jnp.sum(widened * widened, axis=1), "tp")
    mean_sq = square_tot[:, None] / MODEL_WIDTH
    normed = (widened * lax.rsqrt(mean_sq + 1e-05) * norm_gain.astype(jnp.float32)[None, :]).astype(
        jnp.bfloat16
    )
    return (updated, normed)


def solution(mesh):
    in_specs = (
        P(("group", "dp"), None, "tp"),
        P(("group", "dp"), "tp"),
        P("tp", None),
        P(None, "tp", None),
        P(None, None, "tp"),
        P(("group", "dp")),
        P(),
        P("tp"),
    )
    out_specs = (P(("group", "dp"), "tp"), P(("group", "dp"), "tp"))
    return jax.shard_map(
        on_device, mesh=mesh, in_specs=in_specs, out_specs=out_specs, check_vma=False
    )
```

profile of v0, /device:TPU:0, one launch (start us, length us, event | category | flops | bytes accessed | tf_op | source)
XLA Modules:
  0.0 445.6 jit_solution(16633648931576871459)
XLA Ops:
  7.2 0.0 copy-start
  7.2 0.0 copy-start.3
  7.2 0.0 copy-start.2
  7.2 0.0 all-reduce.2.cloned.1.call-start
  7.2 15.7 %fusion.16 = (bf16[1024,1,1792]{2,1,0:T(2,128)(2,1)}, bf16[1024,1,1792]{2,1,0:T(2,128)(2,1)}) fusion(bf16[1024,2,1792]{2,1,0:T(2,128)(2,1)} %param.8), kind=kLoop, calls=%fused_computation.32 | loop fusion | bytes 14680064 | tf_op jit(solution)/shard_map/slice | solution.py:22
  23.0 0.0 copy-done.3
  23.0 0.0 copy-done.2
  23.0 0.1 select_reduce_fusion
  23.1 11.3 %copy_convert_fusion = (f32[1024,1,1792]{2,0,1:T(8,128)}, f32[1024,1,1792]{2,0,1:T(8,128)}) fusion(bf16[1024,1,1792]{2,1,0:T(2,128)(2,1)} %get-tuple-element.5, bf16[1024,1,1792]{2,1,0:T(2,128)(2,1)} %get-tuple-element.4), kind=kLoop, calls=%fused_computation.18 | loop fusion | flops 3670016 | bytes 22020096 | tf_op jit(solution)/shard_map/convert_element_type | solution.py:23
  34.4 6.0 %gather_fusion = bf16[32,1792,64]{1,2,0:T(8,128)(2,1)} fusion(bf16[16,1792,64]{1,2,0:T(8,128)(2,1)} %param.11, s32[1024]{0:T(1024)S(1)} %pad_clamp_fusion), kind=kCustom, calls=%fused_computation | custom fusion | bytes 14680192 | tf_op jit(solution)/shard_map/gather | solution.py:34
  40.4 10.0 %fusion.11 = bf16[32,32,64]{2,1,0:T(8,128)(2,1)} fusion(bf16[32,1792,64]{1,2,0:T(8,128)(2,1)} %gather_fusion, f32[32,32,1792]{2,1,0:T(8,128)} %bitcast.34, f32[32,32,1792]{2,1,0:T(8,128)} %bitcast.35), kind=kOutput, calls=%fused_computation.23 | convolution fusion | flops 245956608 | bytes 22151168 | tf_op jit(solution)/shard_map/bkf,bfr->bkr/dot_general | solution.py:35
  50.4 0.0 all-reduce.2.cloned.1.call-update
  50.4 0.2 reduce-scatter.2.cloned.1.call-start
  50.6 42.0 %convolution_convert_fusion = bf16[1024,8192]{1,0:T(8,128)(2,1)} fusion(bf16[1792,8192]{1,0:T(8,128)(2,1)} %param.10, bf16[1024,1,1792]{2,1,0:T(2,128)(2,1)} %get-tuple-element.4, bf16[1024,1,1792]{2,1,0:T(2,128)(2,1)} %get-tuple-element.5), kind=kOutput, calls=%fused_computation.2 | convolution fusion | flops 30087839744 | bytes 53477376 | tf_op jit(solution)/shard_map/dot_general | solution.py:37
  92.7 0.0 reduce-scatter.2.cloned.1.call-update
  92.7 0.0 copy-done
  92.7 0.0 copy-start.1
  92.7 2.9 gather_fusion.1
  95.6 0.0 copy-done.1
  95.6 28.3 %all-reduce.2.cloned.1.call-done = bf16[32,32,64]{2,1,0:T(8,128)(2,1)} async-done(((bf16[32,32,64]{2,1,0:T(8,128)(2,1)}), bf16[32,32,64]{2,1,0:T(8,128)(2,1)}) %all-reduce.2.cloned.1.call-update) | async-done | bytes 131088 | tf_op jit(solution)/shard_map/psum | solution.py:36
  123.8 5.0 %convolution_multiply_fusion = f32[32,32,1024]{2,1,0:T(8,128)} fusion(bf16[32,32,64]{2,1,0:T(8,128)(2,1)} %all-reduce.2.cloned.1.call-done, bf16[32,64,1024]{2,1,0:T(8,128)(2,1)} %gather_fusion.1), kind=kOutput, calls=%fused_computation.22 | convolution fusion | flops 135266304 | bytes 8519680 | tf_op jit(solution)/shard_map/xcf,xfe->xce/dot_general | solution.py:42
  128.9 281.3 %reduce-scatter.2.cloned.1.call-done = bf16[1024,1024]{1,0:T(8,128)(2,1)} async-done(((bf16[1024,8192]{1,0:T(8,128)(2,1)}), bf16[1024,1024]{1,0:T(8,128)(2,1)}) %reduce-scatter.2.cloned.1.call-update) | async-done | bytes 2097168 | tf_op jit(solution)/shard_map/reduce_scatter | solution.py:38
  410.2 5.6 %fusion.4 = (f32[1024]{0:T(1024)S(1)}, bf16[1024,1024]{1,0:T(8,128)(2,1)}) fusion(f32[32,32,1024]{2,1,0:T(8,128)} %convolution_multiply_fusion, bf16[1024,1024]{1,0:T(8,128)(2,1)} %reduce-scatter.2.cloned.1.call-done, bf16[1024,1024]{1,0:T(8,128)(2,1)} %param.9), kind=kLoop, calls=%fused_computation.13 | loop fusion | flops 8387584 | bytes 10489856 | tf_op jit(solution)/shard_map/reduce_sum | solution.py:50
  415.8 19.4 %psum.15 = f32[1024]{0:T(1024)S(1)} all-reduce(f32[1024]{0:T(1024)S(1)} %get-tuple-element.2), channel_id=1, replica_groups=mesh['group'=2,'tp'=8,'dp'=2] {'tp'}, use_global_device_ids=true, to_apply=%region_4.5 | all-reduce | flops 1024 | bytes 8192 | tf_op jit(solution)/shard_map/psum | solution.py:50
  435.3 3.5 fusion.6
  (4 shorter events, 0.0 us)
Async XLA Ops:
  7.2 85.5 %copy-start = (bf16[16,64,1024]{2,1,0:T(8,128)(2,1)S(1)}, bf16[16,64,1024]{2,1,0:T(8,128)(2,1)}, u32[]{:S(2)}) copy-start(bf16[16,64,1024]{2,1,0:T(8,128)(2,1)} %param.12) | copy-start | bytes 6291460
  7.2 15.8 %copy-start.3 = (s32[32]{0:T(128)S(1)}, s32[32]{0:T(128)}, u32[]{:S(2)}) copy-start(s32[32]{0:T(128)} %param.13) | copy-start | bytes 388
  7.2 15.8 %copy-start.2 = (s32[16]{0:T(128)S(1)}, s32[16]{0:T(128)}, u32[]{:S(2)}) copy-start(s32[16]{0:T(128)} %param.14) | copy-start | bytes 196
  7.2 116.6 %all-reduce.2.cloned.1.call-start = ((), (), s32[]{:S(2)}) async-start(), calls=%async_computation.2 | async-start | bytes 524288 | tf_op jit(solution)/shard_map/psum | solution.py:36
  50.4 359.8 %reduce-scatter.2.cloned.1.call-start = ((), (), s32[]{:S(2)}) async-start(), calls=%async_computation.1 | async-start | bytes 18874368 | tf_op jit(solution)/shard_map/reduce_scatter | solution.py:38
  92.7 2.9 copy-start.1
Sparse Core Ops, SparseCore 0:
  50.5 73.2 all-reduce.1
  128.1 282.0 reduce-scatter.1
where the time goes:
time: 446 us
  waiting for transfers between devices  310 us (70%)
  matrix products  57.1 us (13%)
  local copies, waits for them, and re-layouts  24.6 us (6%)
  other arithmetic  20.5 us (5%)
  blocking collectives  19.4 us (4%)
  between operations  14.1 us (3%)
    reduce_scatter x1, waiting for transfers between devices, on_device(): lax.psum_scatter(base_term.astype(jnp.bfloat16), 'tp', scatter_dimension=...  281 us
    dot_general x1, matrix products, on_device(): base_term = jnp.dot(hidden, down_weight, preferred_element_type=jnp.float32)  42 us
    psum x1, waiting for transfers between devices, on_device(): shrunk_rows = lax.psum(rank_terms.astype(jnp.bfloat16), 'tp')  28.3 us
    psum x1, blocking collectives, on_device(): square_tot = lax.psum(jnp.sum(widened * widened, axis=1), 'tp')  19.4 us
    slice x1, local copies, waits for them, and re-layouts, on_device(): gate_val = gate_up[:, 0, :].astype(jnp.float32)  15.7 us
    convert_element_type x1, other arithmetic, on_device(): up_val = gate_up[:, 1, :].astype(jnp.float32)  11.3 us
    dot_general x1, matrix products, on_device(): jnp.einsum('bkf,bfr->bkr', stacked, picked, preferred_element_type=jnp.fl...  10 us
  transfers between devices with their start and end apart: 2, of which 2 were waited for; matrix products, arithmetic and copies ran while one was open for 11% of the time, Pallas kernels for 0%

commit v1 on v0

--- a/solution.py
+++ b/solution.py
@@ -1,15 +1,251 @@
+import functools
+
 import jax
 import jax.numpy as jnp
 from jax import lax
+from jax.experimental import pallas as pl
+from jax.experimental.pallas import tpu as pltpu
 from jax.sharding import PartitionSpec as P
 
 MODEL_WIDTH = 8192
+CHUNK_ROWS = 128
+COL_TILE = 256
 
 
 adapter_scale = 0.5
 
 
+def project_kernel(depth, pair, chunks, h_ref, w_hbm, out_ref, w_vmem, outgoing, held, landed, acc,
+                   w_sem, pair_send, pair_recv, line_send, line_recv):
+    me = lax.axis_index("tp")
+    pos = me // pair
+    side = me % pair
+    rows = CHUNK_ROWS
+    width = acc.shape[1]
+    tile = min(COL_TILE, width)
+    toward = 2 * (pos // (depth // 2)) - 1
+
+    def target(j):
+        return (pos + toward * (1 + j) + depth) % depth
+
+    def w_copy(block):
+        return pltpu.make_async_copy(
+            w_hbm.at[:, pl.ds(pl.multiple_of(block * width, width), width)],
+            w_vmem.at[block], w_sem.at[block])
+
+    def pair_copy(chunk, dest):
+        return pltpu.make_async_remote_copy(
+            src_ref=outgoing.at[chunk % 2, dest], dst_ref=held.at[chunk, dest],
+            send_sem=pair_send.at[chunk, dest], recv_sem=pair_recv.at[chunk, dest],
+            device_id={"tp": pos * pair + (1 - side)}, device_id_type=pl.DeviceIdType.MESH)
+
+    def line_copy(chunk, dest, slot, to):
+        return pltpu.make_async_remote_copy(
+            src_ref=held.at[chunk, dest], dst_ref=landed.at[chunk, slot],
+            send_sem=line_send.at[chunk, dest], recv_sem=line_recv.at[chunk, slot],
+            device_id={"tp": to * pair + side}, device_id_type=pl.DeviceIdType.MESH)
+
+    barrier = pltpu.get_barrier_semaphore()
+    if pair > 1:
+        pl.semaphore_signal(barrier, inc=1, device_id={"tp": pos * pair + (1 - side)},
+                            device_id_type=pl.DeviceIdType.MESH)
+
+    @pl.when(pos > 0)
+    def _():
+        pl.semaphore_signal(barrier, inc=1, device_id={"tp": me - pair},
+                            device_id_type=pl.DeviceIdType.MESH)
+
+    @pl.when(pos < depth - 1)
+    def _():
+        pl.semaphore_signal(barrier, inc=1, device_id={"tp": me + pair},
+                            device_id_type=pl.DeviceIdType.MESH)
+
+    def start_w(j, _):
+        if pair > 1:
+            w_copy(target(j) * pair + (1 - side)).start()
+        return 0
+
+    lax.fori_loop(0, depth, start_w, 0)
+
+    def start_w_own(j, _):
+        w_copy(target(j) * pair + side).start()
+        return 0
+
+    lax.fori_loop(0, depth, start_w_own, 0)
+
+    pl.semaphore_wait(
+        barrier, pair - 1 + jnp.minimum(pos, 1) + jnp.minimum(depth - 1 - pos, 1))
+
+    def lines(chunk):
+        return pl.ds(pl.multiple_of(chunk * rows, rows), rows)
+
+    def offer(chunk):
+        def one(j, _):
+            dest = target(j)
+            block = dest * pair + (1 - side)
+
+            @pl.when(chunk == 0)
+            def _():
+                w_copy(block).wait()
+
+            @pl.when(chunk >= 2)
+            def _():
+                pair_copy(chunk - 2, dest).wait_send()
+
+            def col(n, _):
+                cols = pl.ds(pl.multiple_of(n * tile, tile), tile)
+                outgoing[chunk % 2, dest, :, cols] = jnp.dot(
+                    h_ref[lines(chunk), :], w_vmem[block, :, cols],
+                    preferred_element_type=jnp.float32).astype(jnp.bfloat16)
+                return 0
+
+            lax.fori_loop(0, width // tile, col, 0)
+            pair_copy(chunk, dest).start()
+            return 0
+
+        lax.fori_loop(0, depth, one, 0)
+
+    def gather_own(chunk, dest):
+        block = dest * pair + side
+
+        @pl.when(chunk == 0)
+        def _():
+            w_copy(block).wait()
+
+        def col(n, _):
+            cols = pl.ds(pl.multiple_of(n * tile, tile), tile)
+            acc[:, cols] = jnp.dot(h_ref[lines(chunk), :], w_vmem[block, :, cols],
+                                   preferred_element_type=jnp.float32)
+            return 0
+
+        lax.fori_loop(0, width // tile, col, 0)
+        if pair > 1:
+            pair_copy(chunk, dest).wait_recv()
+            acc[...] += held[chunk, dest].astype(jnp.float32)
+
+    def take(chunk, slot):
+        line_copy(chunk, 0, slot, pos).wait_recv()
+        acc[...] += landed[chunk, slot].astype(jnp.float32)
+
+    def forward(chunk, dest, up):
+        gather_own(chunk, dest)
+        if up:
+            @pl.when(pos > 0)
+            def _():
+                take(chunk, dest)
+            held[chunk, dest] = acc[...].astype(jnp.bfloat16)
+            line_copy(chunk, dest, dest, pos + 1).start()
+        else:
+            @pl.when(pos < depth - 1)
+            def _():
+                take(chunk, dest)
+            held[chunk, dest] = acc[...].astype(jnp.bfloat16)
+            slot = dest + (depth - dest) * (1 - jnp.minimum(pos - 1 - dest, 1))
+            line_copy(chunk, dest, slot, pos - 1).start()
+
+    def send_up(chunk):
+        def one(j, _):
+            forward(chunk, depth - 1 - j, True)
+            return 0
+
+        lax.fori_loop(0, depth - 1 - pos, one, 0)
+
+    def send_down(chunk):
+        def one(j, _):
+            forward(chunk, j, False)
+            return 0
+
+        lax.fori_loop(0, pos, one, 0)
+
+    def keep(chunk):
+        gather_own(chunk, pos)
+
+        @pl.when(pos > 0)
+        def _():
+            take(chunk, pos)
+
+        @pl.when(pos < depth - 1)
+        def _():
+            take(chunk, depth)
+
+        out_ref[lines(chunk), :] = acc[...]
+
+    def step(k, _):
+        if pair > 1:
+            @pl.when(k < chunks)
+            def _():
+                offer(k)
+
+        upward = k - 1 - pos
+        downward = k - depth + pos
+
+        @pl.when(jnp.logical_and(upward >= 0, upward < chunks))
+        def _():
+            send_up(upward)
+
+        @pl.when(jnp.logical_and(downward >= 0, downward < chunks))
+        def _():
+            send_down(downward)
+
+        last = jnp.minimum(upward, downward)
+
+        @pl.when(jnp.logical_and(last >= 0, last < chunks))
+        def _():
+            keep(last)
+        return 0
+
+    lax.fori_loop(0, chunks + depth, step, 0)
+
+    def finish(chunk, _):
+        def one(dest, _):
+            @pl.when(dest != pos)
+            def _():
+                line_copy(chunk, dest, dest, pos).wait_send()
+            if pair > 1:
+                @pl.when(chunk >= chunks - 2)
+                def _():
+                    pair_copy(chunk, dest).wait_send()
+            return 0
+
+        lax.fori_loop(0, depth, one, 0)
+        return 0
+
+    lax.fori_loop(0, chunks, finish, 0)
+
+
+def project(hidden, down_weight, depth, pair):
+    count, inner = hidden.shape
+    width = down_weight.shape[1] // (depth * pair)
+    chunks = count // CHUNK_ROWS
+    block = (CHUNK_ROWS, width)
+    return pl.pallas_call(
+        functools.partial(project_kernel, depth, pair, chunks),
+        out_shape=jax.ShapeDtypeStruct((count, width), jnp.float32),
+        in_specs=[pl.BlockSpec(memory_space=pltpu.VMEM), pl.BlockSpec(memory_space=pl.ANY)],
+        out_specs=pl.BlockSpec(memory_space=pltpu.VMEM),
+        scratch_shapes=[
+            pltpu.VMEM((depth * pair, inner, width), jnp.bfloat16),
+            pltpu.VMEM((2, depth if pair > 1 else 1) + block, jnp.bfloat16),
+            pltpu.VMEM((chunks, depth) + block, jnp.bfloat16),
+            pltpu.VMEM((chunks, depth + 1) + block, jnp.bfloat16),
+            pltpu.VMEM(block, jnp.float32),
+            pltpu.SemaphoreType.DMA((depth * pair,)),
+            pltpu.SemaphoreType.DMA((chunks, depth)),
+            pltpu.SemaphoreType.DMA((chunks, depth)),
+            pltpu.SemaphoreType.DMA((chunks, depth)),
+            pltpu.SemaphoreType.DMA((chunks, depth + 1)),
+        ],
+        compiler_params=pltpu.CompilerParams(
+            collective_id=0, has_side_effects=True, vmem_limit_bytes=60 * 1024 * 1024),
+        cost_estimate=pl.CostEstimate(
+            flops=2 * count * inner * down_weight.shape[1],
+            bytes_accessed=200_000_000, transcendentals=0),
+    )(hidden, down_weight)
+
+
 def on_device(
+    depth,
+    pair,
     gate_up,
     residual,
     down_weight,
@@ -26,6 +262,7 @@
     blocks = block_adapter.shape[0]
     block_rows = count_of_rows // blocks
     adapters = adapter_slot.shape[0]
+    rank = shrink_weight.shape[2]
     column_count = expand_weight.shape[2]
     adapter_range = jnp.arange(adapters, dtype=jnp.int32)
     chosen = block_adapter[:, None] == adapter_range[None, :]
@@ -34,15 +271,13 @@
     picked = shrink_weight[slot_ids]
     rank_terms = jnp.einsum("bkf,bfr->bkr", stacked, picked, preferred_element_type=jnp.float32)
     shrunk_rows = lax.psum(rank_terms.astype(jnp.bfloat16), "tp")
-    base_term = jnp.dot(hidden, down_weight, preferred_element_type=jnp.float32)
-    projection_sum = lax.psum_scatter(
-        base_term.astype(jnp.bfloat16), "tp", scatter_dimension=1, tiled=True
-    ).astype(jnp.float32)
-    expand_selected = expand_weight[slot_ids]
-    adapter_term = jnp.einsum(
-        "xcf,xfe->xce", shrunk_rows, expand_selected, preferred_element_type=jnp.float32
-    )
-    adapter_term = adapter_term.reshape(count_of_rows, column_count)
+    projection_sum = project(hidden, down_weight, depth, pair)
+    at_slot = (slot_ids[:, None] == adapter_range[None, :]).astype(jnp.bfloat16)
+    spread = (shrunk_rows[:, :, None, :] * at_slot[:, None, :, None]).reshape(
+        count_of_rows, adapters * rank)
+    adapter_term = jnp.dot(
+        spread, expand_weight.reshape(adapters * rank, column_count),
+        preferred_element_type=jnp.float32)
     updated = (residual.astype(jnp.float32) + projection_sum + adapter_scale * adapter_term).astype(
         jnp.bfloat16
     )
@@ -67,6 +302,9 @@
         P("tp"),
     )
     out_specs = (P(("group", "dp"), "tp"), P(("group", "dp"), "tp"))
+    pair = max(1, 4 // mesh.shape["group"])
+    depth = mesh.shape["tp"] // pair
     return jax.shard_map(
-        on_device, mesh=mesh, in_specs=in_specs, out_specs=out_specs, check_vma=False
+        functools.partial(on_device, depth, pair),
+        mesh=mesh, in_specs=in_specs, out_specs=out_specs, check_vma=False
     )

time: 446 us -> 309 us (0.69)
  waiting for transfers between devices: 310 us -> 0.02 us
  Pallas kernels: 0 us -> 203 us
  matrix products: 57.1 us -> 17.4 us
  other arithmetic: 20.5 us -> 28.6 us
    reduce_scatter x1 -> x0, waiting for transfers between devices: 281 us -> none  [on_device(): lax.psum_scatter(base_term.astype(jnp.bfloat16), 'tp', scatter_dimension=...]
    pallas_call x0 -> x1, Pallas kernels: none -> 203 us  [project(): pl.pallas_call(functools.partial(project_kernel, depth, pair, chunks), ou...]
    dot_general x2 -> x1, matrix products: 47.1 us -> 7.38 us  [on_device(): jnp.dot(spread, expand_weight.reshape(adapters * rank, column_count), pre...]
    psum x1, waiting for transfers between devices: 28.3 us -> 0.01 us  [on_device(): shrunk_rows = lax.psum(rank_terms.astype(jnp.bfloat16), 'tp')]
    convert_element_type x0 -> x2, other arithmetic: none -> 10.3 us  [the longest x1 10.2 us: on_device(): hidden = (jax.nn.silu(gate_val) * up_val).astype(jnp.bfloat16)]
    mul x0 -> x1, local copies, waits for them, and re-layouts: none -> 6.49 us  [on_device(): shrunk_rows[:, :, None, :] * at_slot[:, None, :, None]]
    reduce_sum x1 -> x0, other arithmetic: 5.63 us -> none  [on_device(): square_tot = lax.psum(jnp.sum(widened * widened, axis=1), 'tp')]
  transfers between devices with their start and end apart: 2 -> 1, of which waited for: 2 -> 0; matrix products, arithmetic and copies ran while one was open for 11% -> 3% of each run, Pallas kernels for 0% -> 66%
where the time goes in v1:
time: 309 us
  Pallas kernels  203 us (66%)
  other arithmetic  28.6 us (9%)
  local copies, waits for them, and re-layouts  27.9 us (9%)
  blocking collectives  17.8 us (6%)
  matrix products  17.4 us (6%)
  between operations  14.1 us (5%)
    pallas_call x1, Pallas kernels, project(): pl.pallas_call(functools.partial(project_kernel, depth, pair, chunks), ou...  203 us
    psum x1, blocking collectives, on_device(): square_tot = lax.psum(jnp.sum(widened * widened, axis=1), 'tp')  17.8 us
    slice x1, local copies, waits for them, and re-layouts, on_device(): up_val = gate_up[:, 1, :].astype(jnp.float32)  15.4 us
    convert_element_type x1, other arithmetic, on_device(): up_val = gate_up[:, 1, :].astype(jnp.float32)  11.3 us
    convert_element_type x1, other arithmetic, on_device(): hidden = (jax.nn.silu(gate_val) * up_val).astype(jnp.bfloat16)  10.2 us
    dot_general x1, matrix products, on_device(): jnp.einsum('bkf,bfr->bkr', stacked, picked, preferred_element_type=jnp.fl...  10 us
    dot_general x1, matrix products, on_device(): jnp.dot(spread, expand_weight.reshape(adapters * rank, column_count), pre...  7.38 us
    mul x1, local copies, waits for them, and re-layouts, on_device(): shrunk_rows[:, :, None, :] * at_slot[:, None, :, None]  6.49 us
  transfers between devices with their start and end apart: 1, of which 0 were waited for; matrix products, arithmetic and copies ran while one was open for 3% of the time, Pallas kernels for 66%

profile of v1, /device:TPU:0, one launch (start us, length us, event | category | flops | bytes accessed | tf_op | source)
XLA Modules:
  0.0 308.9 jit_solution(3885608072536068208)
XLA Ops:
  7.2 0.0 copy-start
  7.2 0.0 copy-start.3
  7.2 0.0 copy-start.2
  7.2 0.0 all-reduce.2.cloned.1.call-start
  7.2 15.4 %fusion.12 = (bf16[1024,1,1792]{2,1,0:T(2,128)(2,1)}, bf16[1024,1,1792]{2,1,0:T(2,128)(2,1)}) fusion(bf16[1024,2,1792]{2,1,0:T(2,128)(2,1)} %param.8), kind=kLoop, calls=%fused_computation.29 | loop fusion | bytes 14680064 | tf_op jit(solution)/shard_map/slice | solution.py:259
  22.7 0.0 copy-done.3
  22.7 0.0 copy-done.2
  22.7 0.1 select_reduce_fusion
  22.8 11.3 %copy_convert_fusion = (f32[1024,1,1792]{2,0,1:T(8,128)}, f32[1024,1,1792]{2,0,1:T(8,128)}) fusion(bf16[1024,1,1792]{2,1,0:T(2,128)(2,1)} %get-tuple-element.2, bf16[1024,1,1792]{2,1,0:T(2,128)(2,1)} %get-tuple-element.3), kind=kLoop, calls=%fused_computation.15 | loop fusion | flops 3670016 | bytes 22020096 | tf_op jit(solution)/shard_map/convert_element_type | solution.py:259
  34.1 6.0 %gather_fusion = bf16[32,1792,64]{1,2,0:T(8,128)(2,1)} fusion(bf16[16,1792,64]{1,2,0:T(8,128)(2,1)} %param.11, s32[1024]{0:T(1024)S(1)} %pad_clamp_fusion), kind=kCustom, calls=%fused_computation | custom fusion | bytes 14680192 | tf_op jit(solution)/shard_map/gather | solution.py:271
  40.1 10.0 %fusion.8 = bf16[32,32,64]{2,1,0:T(8,128)(2,1)} fusion(bf16[32,1792,64]{1,2,0:T(8,128)(2,1)} %gather_fusion, f32[32,32,1792]{2,1,0:T(8,128)} %bitcast.30, f32[32,32,1792]{2,1,0:T(8,128)} %bitcast.31), kind=kOutput, calls=%fused_computation.19 | convolution fusion | flops 245956608 | bytes 22151168 | tf_op jit(solution)/shard_map/bkf,bfr->bkr/dot_general | solution.py:272
  50.1 0.0 all-reduce.2.cloned.1.call-update
  50.1 0.0 copy-start.1
  50.1 10.2 %fusion.h_ref = bf16[1024,1792]{1,0:T(8,128)(2,1)} fusion(bf16[1024,1,1792]{2,1,0:T(2,128)(2,1)} %get-tuple-element.3, bf16[1024,1,1792]{2,1,0:T(2,128)(2,1)} %get-tuple-element.2), kind=kLoop, calls=%fused_computation.2 | loop fusion | flops 14680064 | bytes 11010048 | tf_op jit(solution)/shard_map/convert_element_type | solution.py:260
  60.4 0.0 copy-done.1
  60.4 203.1 %shard_map.95 = f32[1024,1024]{1,0:T(8,128)} custom-call(bf16[1024,1792]{1,0:T(8,128)(2,1)} %fusion.h_ref, bf16[1792,8192]{1,0:T(8,128)(2,1)} %w_hbm.1), custom_call_target="tpu_custom_call" | custom-call | flops 30064771072 | bytes 200000000 | tf_op jit(solution)/shard_map/pallas_call | solution.py:221
  263.5 0.1 fusion.9
  263.5 0.0 all-reduce.2.cloned.1.call-done
  263.5 3.4 %broadcast_multiply_fusion = bf16[32,32,16,64]{3,2,1,0:T(8,128)(2,1)} fusion(bf16[32,16]{1,0:T(8,128)(2,1)S(1)} %fusion.9, bf16[32,32,64]{2,1,0:T(8,128)(2,1)} %all-reduce.2.cloned.1.call-done), kind=kLoop, calls=%fused_computation.18 | loop fusion | flops 1048576 | bytes 2229248 | tf_op jit(solution)/shard_map/mul | solution.py:276
  266.9 6.5 %mul.68 = bf16[1024,1024]{1,0:T(8,128)(2,1)} reshape(bf16[32,32,16,64]{3,2,1,0:T(8,128)(2,1)} %broadcast_multiply_fusion) | data formatting | bytes 4194304 | tf_op jit(solution)/shard_map/mul | solution.py:276
  273.4 0.0 copy-done
  273.4 7.4 %fusion.4 = (f32[1024]{0:T(1024)S(1)}, bf16[1024,1024]{1,0:T(8,128)(2,1)}) fusion(bf16[1024,1024]{1,0:T(8,128)(2,1)} %mul.68, bf16[1024,1024]{1,0:T(8,128)(2,1)S(1)} %bitcast.29, f32[1024,1024]{1,0:T(8,128)} %shard_map.95, bf16[1024,1024]{1,0:T(8,128)(2,1)} %param.9), kind=kOutput, calls=%fused_computation.11 | convolution fusion | flops 2155871232 | bytes 12587008 | tf_op jit(solution)/shard_map/dot_general | solution.py:278
  280.8 17.8 %psum.15 = f32[1024]{0:T(1024)S(1)} all-reduce(f32[1024]{0:T(1024)S(1)} %get-tuple-element.4), channel_id=1, replica_groups=mesh['group'=2,'tp'=8,'dp'=2] {'tp'}, use_global_device_ids=true, to_apply=%region_3.4 | all-reduce | flops 1024 | bytes 8192 | tf_op jit(solution)/shard_map/psum | solution.py:285
  298.6 3.5 %fusion.6 = bf16[1024,1024]{1,0:T(8,128)(2,1)} fusion(bf16[1024,1024]{1,0:T(8,128)(2,1)} %get-tuple-element.5, f32[1024]{0:T(1024)S(1)} %convert_element_type.69, f32[1024]{0:T(1024)S(1)} %add_rsqrt_fusion), kind=kLoop, calls=%fused_computation.13 | loop fusion | flops 4194304 | bytes 4202496 | tf_op jit(solution)/shard_map/convert_element_type | solution.py:287
  (4 shorter events, 0.0 us)
Async XLA Ops:
  7.2 266.2 %copy-start = (bf16[16,64,1024]{2,1,0:T(8,128)(2,1)S(1)}, bf16[16,64,1024]{2,1,0:T(8,128)(2,1)}, u32[]{:S(2)}) copy-start(bf16[16,64,1024]{2,1,0:T(8,128)(2,1)} %param.12) | copy-start | bytes 6291460
  7.2 15.5 %copy-start.3 = (s32[32]{0:T(128)S(1)}, s32[32]{0:T(128)}, u32[]{:S(2)}) copy-start(s32[32]{0:T(128)} %param.13) | copy-start | bytes 388
  7.2 15.5 %copy-start.2 = (s32[16]{0:T(128)S(1)}, s32[16]{0:T(128)}, u32[]{:S(2)}) copy-start(s32[16]{0:T(128)} %param.14) | copy-start | bytes 196
  7.2 256.3 %all-reduce.2.cloned.1.call-start = ((), (), s32[]{:S(2)}) async-start(), calls=%async_computation | async-start | bytes 524288 | tf_op jit(solution)/shard_map/psum | solution.py:273
  50.1 10.3 %copy-start.1 = (bf16[1024]{0:T(1024)(128)(2,1)S(1)}, bf16[1024]{0:T(1024)(128)(2,1)}, u32[]{:S(2)}) copy-start(bf16[1024]{0:T(1024)(128)(2,1)} %param.15) | copy-start | bytes 6148
Sparse Core Ops, SparseCore 0:
  50.2 74.2 all-reduce.1

commit v2 on v1

--- a/solution.py
+++ b/solution.py
@@ -243,6 +243,131 @@
     )(hidden, down_weight)
 
 
+def slot_mask(slot_rows, group, rank):
+    per = 128 // rank
+    lane = lax.broadcasted_iota(jnp.int32, slot_rows.shape, 1) // rank
+    return slot_rows == group * per + lane
+
+
+def hidden_kernel(rank, gate_up_ref, shrink_ref, slot_ref, hidden_ref, rank_ref):
+    gate = gate_up_ref[:, 0, :].astype(jnp.float32)
+    up = gate_up_ref[:, 1, :].astype(jnp.float32)
+    hidden = (jax.nn.silu(gate) * up).astype(jnp.bfloat16)
+    hidden_ref[...] = hidden
+    slot_rows = slot_ref[...]
+    total = jnp.zeros(slot_rows.shape, jnp.float32)
+    terms = lax.dot_general(hidden, shrink_ref[...], (((1,), (1,)), ((), ())),
+                            preferred_element_type=jnp.float32)
+    for group in range(shrink_ref.shape[0] // 128):
+        part = terms[:, group * 128:(group + 1) * 128]
+        total += jnp.where(slot_mask(slot_rows, group, rank), part, 0.0)
+    rank_ref[...] = total.astype(jnp.bfloat16)
+
+
+def hidden_and_rank(gate_up, shrink_flat, slot_rows, rank):
+    count, _, inner = gate_up.shape
+    rows = 128
+    return pl.pallas_call(
+        functools.partial(hidden_kernel, rank),
+        grid=(count // rows,),
+        out_shape=(jax.ShapeDtypeStruct((count, inner), jnp.bfloat16),
+                   jax.ShapeDtypeStruct((count, 128), jnp.bfloat16)),
+        in_specs=[pl.BlockSpec((rows, 2, inner), lambda i: (i, 0, 0)),
+                  pl.BlockSpec(shrink_flat.shape, lambda i: (0, 0)),
+                  pl.BlockSpec((rows, 128), lambda i: (i, 0))],
+        out_specs=(pl.BlockSpec((rows, inner), lambda i: (i, 0)),
+                   pl.BlockSpec((rows, 128), lambda i: (i, 0))),
+        compiler_params=pltpu.CompilerParams(vmem_limit_bytes=48 * 1024 * 1024),
+    )(gate_up, shrink_flat, slot_rows)
+
+
+def norm_kernel(size, rank, proj_ref, residual_ref, rank_ref, slot_ref, expand_ref, gain_ref,
+                updated_ref, normed_ref, mine, others, send_sem, recv_sem):
+    me = lax.axis_index("tp")
+    barrier = pltpu.get_barrier_semaphore()
+
+    def greet(j, _):
+        pl.semaphore_signal(barrier, inc=1, device_id={"tp": (me + j) % size},
+                            device_id_type=pl.DeviceIdType.MESH)
+        return 0
+
+    lax.fori_loop(1, size, greet, 0)
+    groups = expand_ref.shape[0] // 128
+    width = updated_ref.shape[1]
+    blocks = mine.shape[0]
+    for b in range(blocks):
+        rows = slice(b * 128, (b + 1) * 128)
+        slot_rows = slot_ref[rows, :]
+        values = rank_ref[rows, :].astype(jnp.float32)
+        spread = jnp.concatenate(
+            [jnp.where(slot_mask(slot_rows, group, rank), values, 0.0) for group in range(groups)],
+            axis=1).astype(jnp.bfloat16)
+        adapter_term = jnp.dot(spread, expand_ref[...], preferred_element_type=jnp.float32)
+        updated = (residual_ref[rows, :].astype(jnp.float32) + proj_ref[rows, :]
+                   + adapter_scale * adapter_term).astype(jnp.bfloat16)
+        updated_ref[rows, :] = updated
+        widened = updated.astype(jnp.float32)
+        squares = widened * widened
+        part = squares[:, :128]
+        for c in range(1, width // 128):
+            part += squares[:, c * 128:(c + 1) * 128]
+        mine[b:b + 1, :] = jnp.sum(part.T, axis=0, keepdims=True)
+
+    pl.semaphore_wait(barrier, size - 1)
+
+    def copy(j):
+        return pltpu.make_async_remote_copy(
+            src_ref=mine, dst_ref=others.at[j], send_sem=send_sem.at[j], recv_sem=recv_sem.at[j],
+            device_id={"tp": (me + j) % size}, device_id_type=pl.DeviceIdType.MESH)
+
+    def send(j, _):
+        copy(j).start()
+        return 0
+
+    lax.fori_loop(1, size, send, 0)
+
+    def receive(j, total):
+        copy(j).wait_recv()
+        return total + others[j]
+
+    total = lax.fori_loop(1, size, receive, mine[...])
+    scale = lax.rsqrt(total / MODEL_WIDTH + 1e-05)
+    gain = gain_ref[...].astype(jnp.float32)
+    for b in range(blocks):
+        rows = slice(b * 128, (b + 1) * 128)
+        column = jnp.broadcast_to(scale[b:b + 1, :], (128, 128)).T
+        for c in range(width // 128):
+            cols = slice(c * 128, (c + 1) * 128)
+            normed_ref[rows, cols] = (updated_ref[rows, cols].astype(jnp.float32) * column
+                                      * gain[:, cols]).astype(jnp.bfloat16)
+
+    def sent(j, _):
+        copy(j).wait_send()
+        return 0
+
+    lax.fori_loop(1, size, sent, 0)
+
+
+def expand_and_norm(size, rank, proj, residual, rank_rows, slot_rows, expand_flat, gain):
+    count, width = residual.shape
+    blocks = count // 128
+    out = jax.ShapeDtypeStruct((count, width), jnp.bfloat16)
+    return pl.pallas_call(
+        functools.partial(norm_kernel, size, rank),
+        out_shape=(out, out),
+        in_specs=[pl.BlockSpec(memory_space=pltpu.VMEM)] * 6,
+        out_specs=(pl.BlockSpec(memory_space=pltpu.VMEM),) * 2,
+        scratch_shapes=[
+            pltpu.VMEM((blocks, 128), jnp.float32),
+            pltpu.VMEM((size, blocks, 128), jnp.float32),
+            pltpu.SemaphoreType.DMA((size,)),
+            pltpu.SemaphoreType.DMA((size,)),
+        ],
+        compiler_params=pltpu.CompilerParams(
+            collective_id=1, has_side_effects=True, vmem_limit_bytes=48 * 1024 * 1024),
+    )(proj, residual, rank_rows, slot_rows, expand_flat, gain)
+
+
 def on_device(
     depth,
     pair,
@@ -255,39 +380,22 @@
     adapter_slot,
     norm_gain,
 ):
-    gate_val = gate_up[:, 0, :].astype(jnp.float32)
-    up_val = gate_up[:, 1, :].astype(jnp.float32)
-    hidden = (jax.nn.silu(gate_val) * up_val).astype(jnp.bfloat16)
-    count_of_rows, ff_local = hidden.shape
+    count_of_rows, _, ff_local = gate_up.shape
     blocks = block_adapter.shape[0]
-    block_rows = count_of_rows // blocks
-    adapters = adapter_slot.shape[0]
-    rank = shrink_weight.shape[2]
+    adapters, _, rank = shrink_weight.shape
     column_count = expand_weight.shape[2]
     adapter_range = jnp.arange(adapters, dtype=jnp.int32)
     chosen = block_adapter[:, None] == adapter_range[None, :]
     slot_ids = jnp.sum(jnp.where(chosen, adapter_slot[None, :], 0), axis=1)
-    stacked = hidden.reshape(blocks, block_rows, ff_local)
-    picked = shrink_weight[slot_ids]
-    rank_terms = jnp.einsum("bkf,bfr->bkr", stacked, picked, preferred_element_type=jnp.float32)
-    shrunk_rows = lax.psum(rank_terms.astype(jnp.bfloat16), "tp")
+    slot_rows = jnp.broadcast_to(
+        slot_ids[:, None, None], (blocks, count_of_rows // blocks, 128)).reshape(count_of_rows, 128)
+    shrink_flat = shrink_weight.transpose(0, 2, 1).reshape(adapters * rank, ff_local)
+    hidden, rank_terms = hidden_and_rank(gate_up, shrink_flat, slot_rows, rank)
+    shrunk_rows = lax.psum(rank_terms, "tp")
     projection_sum = project(hidden, down_weight, depth, pair)
-    at_slot = (slot_ids[:, None] == adapter_range[None, :]).astype(jnp.bfloat16)
-    spread = (shrunk_rows[:, :, None, :] * at_slot[:, None, :, None]).reshape(
-        count_of_rows, adapters * rank)
-    adapter_term = jnp.dot(
-        spread, expand_weight.reshape(adapters * rank, column_count),
-        preferred_element_type=jnp.float32)
-    updated = (residual.astype(jnp.float32) + projection_sum + adapter_scale * adapter_term).astype(
-        jnp.bfloat16
-    )
-    widened = updated.astype(jnp.float32)
-    square_tot = lax.psum(jnp.sum(widened * widened, axis=1), "tp")
-    mean_sq = square_tot[:, None] / MODEL_WIDTH
-    normed = (widened * lax.rsqrt(mean_sq + 1e-05) * norm_gain.astype(jnp.float32)[None, :]).astype(
-        jnp.bfloat16
-    )
-    return (updated, normed)
+    return tuple(expand_and_norm(
+        depth * pair, rank, projection_sum, residual, shrunk_rows, slot_rows,
+        expand_weight.reshape(adapters * rank, column_count), norm_gain[None, :]))
 
 
 def solution(mesh):

time: 309 us -> 257 us (0.83)
  Pallas kernels: 203 us -> 236 us
  other arithmetic: 28.6 us -> 0.76 us
  local copies, waits for them, and re-layouts: 27.9 us -> 5.76 us
  blocking collectives: 17.8 us -> 0 us
  matrix products: 17.4 us -> 0 us
    pallas_call x0 -> x2, Pallas kernels: none -> 31.8 us  [the longest x1 21.3 us: hidden_and_rank(): pl.pallas_call(functools.partial(hidden_kernel, rank), grid=(count // row...]
    convert_element_type x5 -> x0, other arithmetic: 25.1 us -> none  [the longest x1 11.3 us: on_device(): up_val = gate_up[:, 1, :].astype(jnp.float32)]
    psum x1 -> x0, blocking collectives: 17.8 us -> none  [on_device(): square_tot = lax.psum(jnp.sum(widened * widened, axis=1), 'tp')]
    dot_general x2 -> x0, matrix products: 17.4 us -> none  [the longest x1 10 us: on_device(): jnp.einsum('bkf,bfr->bkr', stacked, picked, preferred_element_type=jnp.fl...]
    slice x1 -> x0, local copies, waits for them, and re-layouts: 15.4 us -> none  [on_device(): up_val = gate_up[:, 1, :].astype(jnp.float32)]
    mul x1 -> x0, local copies, waits for them, and re-layouts: 6.49 us -> none  [on_device(): shrunk_rows[:, :, None, :] * at_slot[:, None, :, None]]
    gather x1 -> x0, local copies, waits for them, and re-layouts: 5.99 us -> none  [on_device(): picked = shrink_weight[slot_ids]]
    unnamed x8, local copies, waits for them, and re-layouts: 0.02 us -> 5.41 us
  transfers between devices with their start and end apart: 1 -> 1, of which waited for: 0 -> 0; matrix products, arithmetic and copies ran while one was open for 3% -> 0% of each run, Pallas kernels for 66% -> 80%
where the time goes in v2:
time: 257 us
  Pallas kernels  236 us (92%)
  between operations  14.1 us (5%)
  local copies, waits for them, and re-layouts  5.76 us (2%)
    pallas_call x1, Pallas kernels, project(): pl.pallas_call(functools.partial(project_kernel, depth, pair, chunks), ou...  204 us
    pallas_call x1, Pallas kernels, hidden_and_rank(): pl.pallas_call(functools.partial(hidden_kernel, rank), grid=(count // row...  21.3 us
    pallas_call x1, Pallas kernels, expand_and_norm(): pl.pallas_call(functools.partial(norm_kernel, size, rank), out_shape=(out...  10.6 us
    unnamed x8, local copies, waits for them, and re-layouts  5.41 us
  transfers between devices with their start and end apart: 1, of which 0 were waited for; matrix products, arithmetic and copies ran while one was open for 0% of the time, Pallas kernels for 80%

profile of v2, /device:TPU:0, one launch (start us, length us, event | category | flops | bytes accessed | tf_op | source)
XLA Modules:
  0.0 256.6 jit_solution(16846680051705904872)
XLA Ops:
  7.2 0.0 all-reduce.2.cloned.1.call-start
  7.2 0.8 select_reduce_fusion
  8.0 0.1 broadcast_in_dim.30
  8.0 0.1 broadcast_in_dim.31
  8.1 0.2 broadcast_in_dim.32.slot_ref
  8.3 21.3 %shard_map.95 = (bf16[1024,1792]{1,0:T(8,128)(2,1)S(1)}, bf16[1024,128]{1,0:T(8,128)(2,1)}) custom-call(bf16[1024,2,1792]{2,1,0:T(2,128)(2,1)} %gate_up_ref.1, bf16[1024,1792]{1,0:T(8,128)(2,1)} %bitcast.4, s32[1024,128]{1,0:T(8,128)S(1)} %broadcast_in_dim.32.slot_ref), custom_call_target="tpu_custom_call" | custom-call | tf_op jit(solution)/shard_map/pallas_call | solution.py:270
  29.6 0.0 copy-start.1
  29.6 1.8 copy-done.1
  31.4 0.0 all-reduce.2.cloned.1.call-update
  31.4 0.0 copy-start.2
  31.4 204.1 %shard_map.96.proj_ref = f32[1024,1024]{1,0:T(8,128)} custom-call(bf16[1024,1792]{1,0:T(8,128)(2,1)} %copy-done.1, bf16[1792,8192]{1,0:T(8,128)(2,1)} %w_hbm.1), custom_call_target="tpu_custom_call" | custom-call | flops 30064771072 | bytes 200000000 | tf_op jit(solution)/shard_map/pallas_call | solution.py:221
  235.5 0.0 copy-done.2
  235.5 0.0 all-reduce.2.cloned.1.call-done.rank_ref
  235.6 0.0 copy-start
  235.6 0.9 copy-done
  236.5 10.6 %shard_map.97 = (bf16[1024,1024]{1,0:T(8,128)(2,1)S(1)}, bf16[1024,1024]{1,0:T(8,128)(2,1)S(1)}) custom-call(f32[1024,1024]{1,0:T(8,128)} %shard_map.96.proj_ref, bf16[1024,1024]{1,0:T(8,128)(2,1)} %residual_ref.1, bf16[1024,128]{1,0:T(8,128)(2,1)S(1)} %copy-done, s32[1024,128]{1,0:T(8,128)S(1)} %broadcast_in_dim.32.slot_ref, bf16[1024,1024]{1,0:T(8,128)(2,1)} %bitcast.5, ...), custom_call_target="tpu_custom_call" | custom-call | tf_op jit(solution)/shard_map/pallas_call | solution.py:355
  247.1 1.3 copy.13
  248.4 1.3 copy.14
  (1 shorter events, 0.0 us)
Async XLA Ops:
  7.2 228.4 %all-reduce.2.cloned.1.call-start = ((), (), s32[]{:S(2)}) async-start(), calls=%async_computation | async-start | bytes 524288 | tf_op jit(solution)/shard_map/psum | solution.py:394
  29.6 1.8 copy-start.1
  31.4 204.1 %copy-start.2 = (bf16[1024]{0:T(1024)(128)(2,1)S(1)}, bf16[1024]{0:T(1024)(128)(2,1)}, u32[]{:S(2)}) copy-start(bf16[1024]{0:T(1024)(128)(2,1)} %param.15) | copy-start | bytes 6148
  235.6 1.0 copy-start
Sparse Core Ops, SparseCore 0:
  31.6 74.5 all-reduce.1

commit v3 on v2

--- a/solution.py
+++ b/solution.py
@@ -16,13 +16,14 @@
 
 
 def project_kernel(depth, pair, chunks, h_ref, w_hbm, out_ref, w_vmem, outgoing, held, landed, acc,
-                   w_sem, pair_send, pair_recv, line_send, line_recv):
+                   w_sem, pair_send, pair_recv, line_send, line_recv, *cross_refs):
     me = lax.axis_index("tp")
     pos = me // pair
     side = me % pair
     rows = CHUNK_ROWS
     width = acc.shape[1]
     tile = min(COL_TILE, width)
+    first = 1 if cross_refs else 0
     toward = 2 * (pos // (depth // 2)) - 1
 
     def target(j):
@@ -45,6 +46,21 @@
             send_sem=line_send.at[chunk, dest], recv_sem=line_recv.at[chunk, slot],
             device_id={"tp": to * pair + side}, device_id_type=pl.DeviceIdType.MESH)
 
+    if cross_refs:
+        cross_held, cross_landed, cross_send, cross_recv = cross_refs
+
+        def cross_copy(dest, slot, to):
+            return pltpu.make_async_remote_copy(
+                src_ref=cross_held.at[dest], dst_ref=cross_landed.at[slot],
+                send_sem=cross_send.at[dest], recv_sem=cross_recv.at[slot],
+                device_id={"tp": to * pair + side}, device_id_type=pl.DeviceIdType.MESH)
+
+        def swap_copy():
+            return pltpu.make_async_remote_copy(
+                src_ref=cross_held.at[pos], dst_ref=held.at[0, pos],
+                send_sem=pair_send.at[0, pos], recv_sem=pair_recv.at[0, pos],
+                device_id={"tp": pos * pair + (1 - side)}, device_id_type=pl.DeviceIdType.MESH)
+
     barrier = pltpu.get_barrier_semaphore()
     if pair > 1:
         pl.semaphore_signal(barrier, inc=1, device_id={"tp": pos * pair + (1 - side)},
@@ -84,11 +100,11 @@
             dest = target(j)
             block = dest * pair + (1 - side)
 
-            @pl.when(chunk == 0)
+            @pl.when(chunk == first)
             def _():
                 w_copy(block).wait()
 
-            @pl.when(chunk >= 2)
+            @pl.when(chunk >= first + 2)
             def _():
                 pair_copy(chunk - 2, dest).wait_send()
 
@@ -105,13 +121,7 @@
 
         lax.fori_loop(0, depth, one, 0)
 
-    def gather_own(chunk, dest):
-        block = dest * pair + side
-
-        @pl.when(chunk == 0)
-        def _():
-            w_copy(block).wait()
-
+    def multiply(chunk, block):
         def col(n, _):
             cols = pl.ds(pl.multiple_of(n * tile, tile), tile)
             acc[:, cols] = jnp.dot(h_ref[lines(chunk), :], w_vmem[block, :, cols],
@@ -119,29 +129,58 @@
             return 0
 
         lax.fori_loop(0, width // tile, col, 0)
+
+    def gather_own(chunk, dest, opening):
+        block = dest * pair + side
+
+        @pl.when(chunk == opening)
+        def _():
+            w_copy(block).wait()
+
+        multiply(chunk, block)
         if pair > 1:
-            pair_copy(chunk, dest).wait_recv()
-            acc[...] += held[chunk, dest].astype(jnp.float32)
+            @pl.when(chunk >= first)
+            def _():
+                pair_copy(chunk, dest).wait_recv()
+                acc[...] += held[chunk, dest].astype(jnp.float32)
 
     def take(chunk, slot):
         line_copy(chunk, 0, slot, pos).wait_recv()
         acc[...] += landed[chunk, slot].astype(jnp.float32)
 
+    def cross_take(slot):
+        cross_copy(0, slot, pos).wait_recv()
+        acc[...] += cross_landed[slot].astype(jnp.float32)
+
+    def below_slot(dest):
+        return dest + (depth - dest) * (1 - jnp.minimum(pos - 1 - dest, 1))
+
     def forward(chunk, dest, up):
-        gather_own(chunk, dest)
+        gather_own(chunk, dest, 0)
+
+        @pl.when(pos > 0 if up else pos < depth - 1)
+        def _():
+            take(chunk, dest)
+
+        held[chunk, dest] = acc[...].astype(jnp.bfloat16)
         if up:
-            @pl.when(pos > 0)
-            def _():
-                take(chunk, dest)
-            held[chunk, dest] = acc[...].astype(jnp.bfloat16)
             line_copy(chunk, dest, dest, pos + 1).start()
         else:
-            @pl.when(pos < depth - 1)
-            def _():
-                take(chunk, dest)
-            held[chunk, dest] = acc[...].astype(jnp.bfloat16)
-            slot = dest + (depth - dest) * (1 - jnp.minimum(pos - 1 - dest, 1))
-            line_copy(chunk, dest, slot, pos - 1).start()
+            line_copy(chunk, dest, below_slot(dest), pos - 1).start()
+        if cross_refs:
+            @pl.when(chunk == 0)
+            def _():
+                multiply(0, dest * pair + (1 - side))
+
+                @pl.when(pos > 0 if up else pos < depth - 1)
+                def _():
+                    cross_take(dest)
+
+                cross_held[dest] = acc[...].astype(jnp.bfloat16)
+                if up:
+                    cross_copy(dest, dest, pos + 1).start()
+                else:
+                    cross_copy(dest, below_slot(dest), pos - 1).start()
 
     def send_up(chunk):
         def one(j, _):
@@ -158,7 +197,7 @@
         lax.fori_loop(0, pos, one, 0)
 
     def keep(chunk):
-        gather_own(chunk, pos)
+        gather_own(chunk, pos, first)
 
         @pl.when(pos > 0)
         def _():
@@ -168,16 +207,36 @@
         def _():
             take(chunk, depth)
 
+        if cross_refs:
+            @pl.when(chunk == 0)
+            def _():
+                swap_copy().wait_recv()
+                acc[...] += held[0, pos].astype(jnp.float32)
+
         out_ref[lines(chunk), :] = acc[...]
+
+    def swap():
+        multiply(0, pos * pair + (1 - side))
+
+        @pl.when(pos > 0)
+        def _():
+            cross_take(pos)
+
+        @pl.when(pos < depth - 1)
+        def _():
+            cross_take(depth)
+
+        cross_held[pos] = acc[...].astype(jnp.bfloat16)
+        swap_copy().start()
 
     def step(k, _):
         if pair > 1:
-            @pl.when(k < chunks)
-            def _():
-                offer(k)
-
-        upward = k - 1 - pos
-        downward = k - depth + pos
+            @pl.when(k + first < chunks)
+            def _():
+                offer(k + first)
+
+        upward = k + first - 1 - pos
+        downward = k + first - depth + pos
 
         @pl.when(jnp.logical_and(upward >= 0, upward < chunks))
         def _():
@@ -188,13 +247,22 @@
             send_down(downward)
 
         last = jnp.minimum(upward, downward)
-
-        @pl.when(jnp.logical_and(last >= 0, last < chunks))
+        if cross_refs:
+            @pl.when(last == 0)
+            def _():
+                swap()
+
+        @pl.when(jnp.logical_and(last >= first, last < chunks))
         def _():
             keep(last)
-        return 0
-
-    lax.fori_loop(0, chunks + depth, step, 0)
+
+        if cross_refs:
+            @pl.when(last == first + 3)
+            def _():
+                keep(0)
+        return 0
+
+    lax.fori_loop(0, chunks + depth - first, step, 0)
 
     def finish(chunk, _):
         def one(dest, _):
@@ -205,12 +273,18 @@
                 @pl.when(chunk >= chunks - 2)
                 def _():
                     pair_copy(chunk, dest).wait_send()
+            if cross_refs:
+                @pl.when(jnp.logical_and(chunk == 0, dest != pos))
+                def _():
+                    cross_copy(dest, dest, pos).wait_send()
             return 0
 
         lax.fori_loop(0, depth, one, 0)
         return 0
 
     lax.fori_loop(0, chunks, finish, 0)
+    if cross_refs:
+        swap_copy().wait_send()
 
 
 def project(hidden, down_weight, depth, pair):
@@ -218,6 +292,12 @@
     width = down_weight.shape[1] // (depth * pair)
     chunks = count // CHUNK_ROWS
     block = (CHUNK_ROWS, width)
+    cross = [] if pair == 1 or chunks < 6 else [
+        pltpu.VMEM((depth,) + block, jnp.bfloat16),
+        pltpu.VMEM((depth + 1,) + block, jnp.bfloat16),
+        pltpu.SemaphoreType.DMA((depth,)),
+        pltpu.SemaphoreType.DMA((depth + 1,)),
+    ]
     return pl.pallas_call(
         functools.partial(project_kernel, depth, pair, chunks),
         out_shape=jax.ShapeDtypeStruct((count, width), jnp.float32),
@@ -234,7 +314,7 @@
             pltpu.SemaphoreType.DMA((chunks, depth)),
             pltpu.SemaphoreType.DMA((chunks, depth)),
             pltpu.SemaphoreType.DMA((chunks, depth + 1)),
-        ],
+        ] + cross,
         compiler_params=pltpu.CompilerParams(
             collective_id=0, has_side_effects=True, vmem_limit_bytes=60 * 1024 * 1024),
         cost_estimate=pl.CostEstimate(

time: 257 us -> 240 us (0.934)
  Pallas kernels: 236 us -> 219 us
    pallas_call x1, Pallas kernels: 204 us -> 187 us  [project(): pl.pallas_call(functools.partial(project_kernel, depth, pair, chunks), ou...]
  transfers between devices with their start and end apart: 1 -> 1, of which waited for: 0 -> 0; matrix products, arithmetic and copies ran while one was open for 0% -> 0% of each run, Pallas kernels for 80% -> 78%
where the time goes in v3:
time: 240 us
  Pallas kernels  219 us (91%)
  between operations  14.1 us (6%)
  local copies, waits for them, and re-layouts  5.76 us (2%)
    pallas_call x1, Pallas kernels, project(): pl.pallas_call(functools.partial(project_kernel, depth, pair, chunks), ou...  187 us
    pallas_call x1, Pallas kernels, hidden_and_rank(): pl.pallas_call(functools.partial(hidden_kernel, rank), grid=(count // row...  21.3 us
    pallas_call x1, Pallas kernels, expand_and_norm(): pl.pallas_call(functools.partial(norm_kernel, size, rank), out_shape=(out...  10.6 us
    unnamed x8, local copies, waits for them, and re-layouts  5.41 us
  transfers between devices with their start and end apart: 1, of which 0 were waited for; matrix products, arithmetic and copies ran while one was open for 0% of the time, Pallas kernels for 78%

profile of v3, /device:TPU:0, one launch (start us, length us, event | category | flops | bytes accessed | tf_op | source)
XLA Modules:
  0.0 239.9 jit_solution(17026080467155381164)
XLA Ops:
  7.2 0.0 all-reduce.2.cloned.1.call-start
  7.2 0.8 select_reduce_fusion
  8.0 0.1 broadcast_in_dim.30
  8.0 0.1 broadcast_in_dim.31
  8.1 0.2 broadcast_in_dim.32.slot_ref
  8.3 21.3 %shard_map.95 = (bf16[1024,1792]{1,0:T(8,128)(2,1)S(1)}, bf16[1024,128]{1,0:T(8,128)(2,1)}) custom-call(bf16[1024,2,1792]{2,1,0:T(2,128)(2,1)} %gate_up_ref.1, bf16[1024,1792]{1,0:T(8,128)(2,1)} %bitcast.4, s32[1024,128]{1,0:T(8,128)S(1)} %broadcast_in_dim.32.slot_ref), custom_call_target="tpu_custom_call" | custom-call | tf_op jit(solution)/shard_map/pallas_call | solution.py:350
  29.6 0.0 copy-start.1
  29.6 1.8 copy-done.1
  31.4 0.0 all-reduce.2.cloned.1.call-update
  31.4 0.0 copy-start.2
  31.4 187.4 %shard_map.96.proj_ref = f32[1024,1024]{1,0:T(8,128)} custom-call(bf16[1024,1792]{1,0:T(8,128)(2,1)} %copy-done.1, bf16[1792,8192]{1,0:T(8,128)(2,1)} %w_hbm.1), custom_call_target="tpu_custom_call" | custom-call | flops 30064771072 | bytes 200000000 | tf_op jit(solution)/shard_map/pallas_call | solution.py:301
  218.8 0.0 copy-done.2
  218.8 0.0 all-reduce.2.cloned.1.call-done.rank_ref
  218.9 0.0 copy-start
  218.9 0.9 copy-done
  219.8 10.6 %shard_map.97 = (bf16[1024,1024]{1,0:T(8,128)(2,1)S(1)}, bf16[1024,1024]{1,0:T(8,128)(2,1)S(1)}) custom-call(f32[1024,1024]{1,0:T(8,128)} %shard_map.96.proj_ref, bf16[1024,1024]{1,0:T(8,128)(2,1)} %residual_ref.1, bf16[1024,128]{1,0:T(8,128)(2,1)S(1)} %copy-done, s32[1024,128]{1,0:T(8,128)S(1)} %broadcast_in_dim.32.slot_ref, bf16[1024,1024]{1,0:T(8,128)(2,1)} %bitcast.5, ...), custom_call_target="tpu_custom_call" | custom-call | tf_op jit(solution)/shard_map/pallas_call | solution.py:435
  230.4 1.3 copy.13
  231.7 1.3 copy.14
  (1 shorter events, 0.0 us)
Async XLA Ops:
  7.2 211.7 %all-reduce.2.cloned.1.call-start = ((), (), s32[]{:S(2)}) async-start(), calls=%async_computation | async-start | bytes 524288 | tf_op jit(solution)/shard_map/psum | solution.py:474
  29.6 1.8 copy-start.1
  31.4 187.4 %copy-start.2 = (bf16[1024]{0:T(1024)(128)(2,1)S(1)}, bf16[1024]{0:T(1024)(128)(2,1)}, u32[]{:S(2)}) copy-start(bf16[1024]{0:T(1024)(128)(2,1)} %param.15) | copy-start | bytes 6148
  218.9 1.0 copy-start
Sparse Core Ops, SparseCore 0:
  31.6 74.9 all-reduce.1
